TPU v7x, 32 devices: a whole 2x2x4 slice. The times are simulated.
32 devices in a mesh: parts: 2 (over x), sec: 16 (over z, y, core).
Axes of the slice: x: 2, y: 2, z: 4, core: 2. Of those that a mesh axis runs over, the one named last changes fastest.
Arguments:
- wave_blocks: bfloat16 [32, 2, 128, 128], P(('parts', 'sec')), parts along dimension 0, may hold values from -6 to 6
- slot_sector: int32 [32], P('parts'), parts along dimension 0, may hold values from 0 to 15, each once
- sector_rows: int32 [32], P('parts'), parts along dimension 0, may hold values from 32 to 128
- sector_cols: int32 [32], P('parts'), parts along dimension 0, may hold values from 32 to 128
- left_ops: bfloat16 [256, 128, 128], P(('parts', 'sec')), parts along dimension 0, may hold values from -0.5 to 0.5
- right_ops: bfloat16 [256, 128, 128], P(('parts', 'sec')), parts along dimension 0, may hold values from -0.5 to 0.5
- term_coef: float32 [256, 16], P(('parts', 'sec')), parts along dimension 0, may hold values from -1.25 to 1.25
- term_shift: int32 [256], P(('parts', 'sec')), parts along dimension 0, may hold values from -2 to 2
Outputs:
- sigma_blocks: bfloat16 [32, 2, 128, 128], P(('parts', 'sec')), parts along dimension 0
There are 2 independent parts, one for each index of `parts`. A program takes and returns all parts, laid end to end along the dimension named above; each array names one. Nothing has to cross between parts.
Inputs may be any that keep to these rules, and one draw needn't show every extreme that they name: slot_sector holds each label 0 .. 15 exactly once.
All inputs are finite; a program needn't handle non-finite values.
Results may differ from a plain program's by a relative error of at most 0.0049.
Values may be sent and summed in bfloat16 or wider, within the bound.
A program may use at most 128 MiB of HBM per device.

v0:
```python
import jax
import jax.numpy as jnp
from jax import lax
from jax.sharding import PartitionSpec as P


def live_cells(labels, sector_rows, sector_cols, left_size, right_size):
    row_live = jnp.arange(left_size, dtype=jnp.int32)[None, :] < sector_rows[labels][:, None]
    col_live = jnp.arange(right_size, dtype=jnp.int32)[None, :] < sector_cols[labels][:, None]
    return (row_live[:, :, None] & col_live[:, None, :])[:, None]


def shards(
    wave_blocks, slot_sector, sector_rows, sector_cols, left_ops, right_ops, term_coef, term_shift
):
    sector_count = slot_sector.shape[0]
    own_count = wave_blocks.shape[0]
    vectors = wave_blocks.shape[1]
    left_size = wave_blocks.shape[2]
    right_size = wave_blocks.shape[3]
    shape_tail = (vectors, left_size, right_size)
    device = lax.axis_index("sec")
    first_slot = device * own_count
    own_labels = lax.dynamic_slice_in_dim(slot_sector, first_slot, own_count)
    own_live = live_cells(own_labels, sector_rows, sector_cols, left_size, right_size)
    masked = jnp.where(own_live, wave_blocks, jnp.zeros((), wave_blocks.dtype))
    term_packs = (left_ops, right_ops, term_coef, term_shift)
    start_sum = jnp.zeros((sector_count,) + shape_tail, jnp.float32)
    source_piece = lax.all_gather(masked, "sec", axis=0, tiled=True)

    def add_term(accumulator, term_pack):
        left_op, right_op, coeff_row, shift_term = term_pack
        target = slot_sector + shift_term
        inside = (target >= 0) & (target < sector_count)
        clipped = jnp.clip(target, 0, sector_count - 1)
        halfway = jnp.einsum(
            "ab,svbc->svac", left_op, source_piece, preferred_element_type=jnp.float32
        ).astype(jnp.bfloat16)
        product_term = jnp.einsum(
            "svac,cd->svad", halfway, right_op, preferred_element_type=jnp.float32
        )
        weight = jnp.where(inside, coeff_row[clipped], 0.0)
        return (accumulator.at[clipped].add(weight[:, None, None, None] * product_term), None)

    updated, unused = lax.scan(add_term, start_sum, term_packs)
    partial_sum = updated[slot_sector]
    slot_live = live_cells(slot_sector, sector_rows, sector_cols, left_size, right_size)
    partial_sum = jnp.where(slot_live, partial_sum, 0.0)
    summed = lax.psum_scatter(partial_sum, "sec", scatter_dimension=0, tiled=True)
    return summed.astype(jnp.bfloat16)


def solution(mesh):
    return jax.shard_map(
        shards,
        mesh=mesh,
        in_specs=(
            P(("parts", "sec"), None, None, None),
            P("parts"),
            P("parts"),
            P("parts"),
            P(("parts", "sec"), None, None),
            P(("parts", "sec"), None, None),
            P(("parts", "sec"), None),
            P(("parts", "sec")),
        ),
        out_specs=P(("parts", "sec"), None, None, None),
        check_vma=False,
    )
```

profile of v0, /device:TPU:0, one launch (start us, length us, event | category | flops | bytes accessed | tf_op | source)
XLA Modules:
  0.0 205.3 jit_solution(12433852559968966691)
XLA Ops:
  6.5 1.3 dynamic_slice.18
  9.8 1.2 dynamic-slice.4
  11.0 1.3 dynamic-slice.5
  12.3 1.3 iota_compare_fusion.2
  13.7 1.5 broadcast_select_fusion.1
  15.9 1.3 gather_fusion.1
  17.2 1.3 gather_fusion.2
  19.0 37.0 %all-gather.2.cloned.1.call-done = bf16[16,2,128,128]{3,2,1,0:T(8,128)(2,1)} async-done(((bf16[1,2,128,128]{3,2,1,0:T(8,128)(2,1)}), bf16[16,2,128,128]{3,2,1,0:T(8,128)(2,1)}) %all-gather.2.cloned.1.call-update) | async-done | bytes 1048592 | tf_op jit(solution)/shard_map/all_gather | solution.py:29
  56.0 1.6 broadcast_in_dim.33
  57.6 74.5 %while.12 = (s32[]{:T(128)}, f32[16,2,128,128]{3,2,1,0:T(8,128)}, s32[8]{0:T(128)S(1)}, s32[16]{0:T(128)S(1)}, f32[8,16]{1,0:T(8,128)}, /*index=5*/bf16[8,128,12...) while((s32[]{:T(128)}, f32[16,2,128,128]{3,2,1,0:T(8,128)}, ...), condition=%wide.region_2.3_spmd, body=%wide.region_0.2_spmd.sunk | while | flops 270009504 | bytes 9508789 | solution.py:45
  58.9 0.7 fusion.21
  60.9 1.5 convolution_multiply_fusion.2
  62.4 4.5 %scatter_fusion = f32[16,2,128,128]{3,2,1,0:T(8,128)} fusion(f32[16,2,128,128]{3,2,1,0:T(8,128)} %get-tuple-element.149, s32[16]{0:T(128)S(1)} %fusion.20, f32[16,2,128,128]{3,2,1,0:T(8,128)S(1)} %convolution_multiply_fusion.2), kind=kCustom, calls=%fused_computation.4.clone.1 | custom fusion | flops 524288 | bytes 6291520 | tf_op jit(solution)/shard_map/while/body/eval_jaxpr/scatter-add | solution.py:43
  68.2 0.7 fusion.21
  70.2 1.5 convolution_multiply_fusion.2
  71.7 4.6 %scatter_fusion = f32[16,2,128,128]{3,2,1,0:T(8,128)} fusion(f32[16,2,128,128]{3,2,1,0:T(8,128)} %get-tuple-element.149, s32[16]{0:T(128)S(1)} %fusion.20, f32[16,2,128,128]{3,2,1,0:T(8,128)S(1)} %convolution_multiply_fusion.2), kind=kCustom, calls=%fused_computation.4.clone.1 | custom fusion | flops 524288 | bytes 6291520 | tf_op jit(solution)/shard_map/while/body/eval_jaxpr/scatter-add | solution.py:43
  79.5 1.5 convolution_multiply_fusion.2
  81.0 4.7 %scatter_fusion = f32[16,2,128,128]{3,2,1,0:T(8,128)} fusion(f32[16,2,128,128]{3,2,1,0:T(8,128)} %get-tuple-element.149, s32[16]{0:T(128)S(1)} %fusion.20, f32[16,2,128,128]{3,2,1,0:T(8,128)S(1)} %convolution_multiply_fusion.2), kind=kCustom, calls=%fused_computation.4.clone.1 | custom fusion | flops 524288 | bytes 6291520 | tf_op jit(solution)/shard_map/while/body/eval_jaxpr/scatter-add | solution.py:43
  88.9 1.5 convolution_multiply_fusion.2
  90.4 4.5 %scatter_fusion = f32[16,2,128,128]{3,2,1,0:T(8,128)} fusion(f32[16,2,128,128]{3,2,1,0:T(8,128)} %get-tuple-element.149, s32[16]{0:T(128)S(1)} %fusion.20, f32[16,2,128,128]{3,2,1,0:T(8,128)S(1)} %convolution_multiply_fusion.2), kind=kCustom, calls=%fused_computation.4.clone.1 | custom fusion | flops 524288 | bytes 6291520 | tf_op jit(solution)/shard_map/while/body/eval_jaxpr/scatter-add | solution.py:43
  98.2 1.5 convolution_multiply_fusion.2
  99.7 4.5 %scatter_fusion = f32[16,2,128,128]{3,2,1,0:T(8,128)} fusion(f32[16,2,128,128]{3,2,1,0:T(8,128)} %get-tuple-element.149, s32[16]{0:T(128)S(1)} %fusion.20, f32[16,2,128,128]{3,2,1,0:T(8,128)S(1)} %convolution_multiply_fusion.2), kind=kCustom, calls=%fused_computation.4.clone.1 | custom fusion | flops 524288 | bytes 6291520 | tf_op jit(solution)/shard_map/while/body/eval_jaxpr/scatter-add | solution.py:43
  107.5 1.5 convolution_multiply_fusion.2
  109.0 4.5 %scatter_fusion = f32[16,2,128,128]{3,2,1,0:T(8,128)} fusion(f32[16,2,128,128]{3,2,1,0:T(8,128)} %get-tuple-element.149, s32[16]{0:T(128)S(1)} %fusion.20, f32[16,2,128,128]{3,2,1,0:T(8,128)S(1)} %convolution_multiply_fusion.2), kind=kCustom, calls=%fused_computation.4.clone.1 | custom fusion | flops 524288 | bytes 6291520 | tf_op jit(solution)/shard_map/while/body/eval_jaxpr/scatter-add | solution.py:43
  116.8 1.5 convolution_multiply_fusion.2
  118.2 4.5 %scatter_fusion = f32[16,2,128,128]{3,2,1,0:T(8,128)} fusion(f32[16,2,128,128]{3,2,1,0:T(8,128)} %get-tuple-element.149, s32[16]{0:T(128)S(1)} %fusion.20, f32[16,2,128,128]{3,2,1,0:T(8,128)S(1)} %convolution_multiply_fusion.2), kind=kCustom, calls=%fused_computation.4.clone.1 | custom fusion | flops 524288 | bytes 6291520 | tf_op jit(solution)/shard_map/while/body/eval_jaxpr/scatter-add | solution.py:43
  126.0 1.5 convolution_multiply_fusion.2
  127.5 4.6 %scatter_fusion = f32[16,2,128,128]{3,2,1,0:T(8,128)} fusion(f32[16,2,128,128]{3,2,1,0:T(8,128)} %get-tuple-element.149, s32[16]{0:T(128)S(1)} %fusion.20, f32[16,2,128,128]{3,2,1,0:T(8,128)S(1)} %convolution_multiply_fusion.2), kind=kCustom, calls=%fused_computation.4.clone.1 | custom fusion | flops 524288 | bytes 6291520 | tf_op jit(solution)/shard_map/while/body/eval_jaxpr/scatter-add | solution.py:43
  132.1 2.3 %gather_fusion.3 = f32[16,2,128,128]{3,2,1,0:T(8,128)S(1)} fusion(f32[16,2,128,128]{3,2,1,0:T(8,128)} %get-tuple-element.47, s32[1024]{0:T(1024)S(1)} %pad_clamp_fusion.1), kind=kCustom, calls=%fused_computation.3 | custom fusion | bytes 4194368 | tf_op jit(solution)/shard_map/gather | solution.py:46
  134.4 1.6 broadcast_select_fusion
  136.0 60.9 %reduce-scatter.2.cloned.1.call-done = f32[1,2,128,128]{3,2,1,0:T(8,128)} async-done(((f32[16,2,128,128]{3,2,1,0:T(8,128)}), f32[1,2,128,128]{3,2,1,0:T(8,128)}) %reduce-scatter.2.cloned.1.call-update) | async-done | bytes 131088 | tf_op jit(solution)/shard_map/reduce_scatter | solution.py:49
  196.9 1.5 convert_element_type.9
  (61 shorter events, 25.9 us)
Async XLA Ops:
  6.5 51.1 %copy-start.1 = (s32[16]{0:T(128)S(1)}, s32[16]{0:T(128)}, u32[]{:S(2)}) copy-start(s32[16]{0:T(128)} %param.11) | copy-start | bytes 196
  6.5 51.1 %copy-start.2 = (s32[8]{0:T(128)S(1)}, s32[8]{0:T(128)}, u32[]{:S(2)}) copy-start(s32[8]{0:T(128)} %param.17) | copy-start | bytes 100
  6.5 49.5 %all-gather.2.cloned.1.call-start = ((), (), s32[]{:S(2)}) async-start(), calls=%async_computation.1 | async-start | bytes 1114112 | tf_op jit(solution)/shard_map/all_gather | solution.py:29
  15.2 181.7 %reduce-scatter.2.cloned.1.call-start = ((), (), s32[]{:S(2)}) async-start(), calls=%async_computation.2 | async-start | bytes 2228224 | tf_op jit(solution)/shard_map/reduce_scatter | solution.py:49
  56.0 1.6 copy-start
Sparse Core Ops, SparseCore 0:
  15.3 40.6 all-gather.1
  136.1 60.7 reduce-scatter.1
where the time goes:
time: 207 us; the launch traced here: 205 us
  waiting for transfers between devices  98 us (47%)
  other arithmetic  54 us (26%)
  local copies, waits for them, and re-layouts  25.9 us (13%)
  between operations  15.4 us (7%)
  matrix products  11.8 us (6%)
    reduce_scatter x1, waiting for transfers between devices, shards(): lax.psum_scatter(partial_sum, 'sec', scatter_dimension=0, tiled=True)  60.9 us
    all_gather x1, waiting for transfers between devices, shards(): source_piece = lax.all_gather(masked, 'sec', axis=0, tiled=True)  37 us
    scatter-add x8, other arithmetic, add_term(): accumulator.at[clipped].add(weight[:, None, None, None] * product_term)  36.4 us
    dot_general x8, matrix products, add_term(): jnp.einsum('svac,cd->svad', halfway, right_op, preferred_element_type=jnp...  11.8 us
    squeeze x8, local copies, waits for them, and re-layouts, shards(): updated, unused = lax.scan(add_term, start_sum, term_packs)  5.58 us
    select_n x8, other arithmetic, add_term(): weight = jnp.where(inside, coeff_row[clipped], 0.0)  5.27 us
    gather x8, local copies, waits for them, and re-layouts, add_term(): weight = jnp.where(inside, coeff_row[clipped], 0.0)  5.25 us
    select_n x8, other arithmetic, add_term(): accumulator.at[clipped].add(weight[:, None, None, None] * product_term)  5.2 us
  transfers between devices with their start and end apart: 2, of which 2 were waited for; matrix products, arithmetic and copies ran while one was open for 2% of the time, Pallas kernels for 0%

commit v1 on v0

v1 whole, which is shorter than its diff:
```python
import functools

import jax
import jax.numpy as jnp
from jax import lax
from jax.experimental import pallas as pl
from jax.experimental.pallas import tpu as pltpu
from jax.sharding import PartitionSpec as P

MESH = pl.DeviceIdType.MESH
REACH = 2


def sigma_kernel(
    n, wave, slots, rows, cols, left, right, coef, shift, coef_far, shift_far,
    out,
    lefts, rights, coef_b, shift_b, coef_in, shift_in, states, half, inverse,
    part_out, part_in, sum_out, sum_in,
    local_sem, ops_send, ops_recv, z_send, z_recv, y_send, y_recv,
    part_send, part_recv, sum_send, sum_recv,
):
    depth = n // 4

    def repeat(begin, end, body, carry):
        if depth > 4:
            return lax.fori_loop(begin, end, body, carry)
        for step in range(begin, end):
            carry = body(step, carry)
        return carry

    terms = left.shape[0]
    size = wave.shape[2]
    me = lax.axis_index("sec")
    core = lax.rem(me, 2)
    y = lax.rem(me // 2, 2)
    z = me // 4

    def core_at(which):
        return 1 - core if which else core

    def row_to(step):
        return lax.rem(z + step, depth)

    def place(step, column, which):
        return (step * 2 + column) * 2 + which

    def slot_of(row, column, which):
        return (row * 2 + (1 - y if column else y)) * 2 + core_at(which)

    def slot_from(step, column, which):
        return slot_of(lax.rem(z + depth - step, depth), column, which)

    def device(row, column, which):
        return {"sec": slot_of(row, column, which)}

    def remote(src, dst, send, recv, target):
        return pltpu.make_async_remote_copy(
            src_ref=src, dst_ref=dst, send_sem=send, recv_sem=recv, device_id=target, device_id_type=MESH
        )

    local = [
        pltpu.make_async_copy(wave.at[0, core], states.at[0], local_sem.at[0]),
        pltpu.make_async_copy(left, lefts.at[pl.ds(0, terms)], local_sem.at[1]),
        pltpu.make_async_copy(right, rights.at[pl.ds(0, terms)], local_sem.at[2]),
    ]
    for copy in local:
        copy.start()

    barrier = pltpu.get_barrier_semaphore()

    def greet(step, carry):
        for which in range(2):
            pl.semaphore_signal(barrier, inc=1, device_id=device(row_to(step), 0, which), device_id_type=MESH)
        return carry

    partner = device(z, 0, 1)
    neighbour = device(z, 1, 0)
    pl.semaphore_signal(barrier, inc=1, device_id=partner, device_id_type=MESH)
    pl.semaphore_signal(barrier, inc=1, device_id=neighbour, device_id_type=MESH)
    repeat(1, depth, greet, 0)
    pl.semaphore_wait(barrier, 2 * depth)

    def z_copy(step, which):
        at = step * 2 + which
        return remote(
            wave.at[0, core_at(which)], states.at[place(step, 0, which)], z_send.at[at], z_recv.at[at],
            device(row_to(step), 0, which),
        )

    def y_copy(step, which):
        at = step * 2 + which
        return remote(
            states.at[place(step, 0, which)], states.at[place(step, 1, which)], y_send.at[at], y_recv.at[at],
            neighbour,
        )

    others = [
        remote(shift_far, shift_in, ops_send.at[0], ops_recv.at[0], partner),
        remote(coef_far, coef_in, ops_send.at[1], ops_recv.at[1], partner),
        remote(left, lefts.at[pl.ds(terms, terms)], ops_send.at[2], ops_recv.at[2], partner),
        remote(right, rights.at[pl.ds(terms, terms)], ops_send.at[3], ops_recv.at[3], partner),
    ]

    def send_column(step, carry):
        for which in range(2):
            z_copy(step, which).start()
        return carry

    repeat(1, depth, send_column, 0)
    z_copy(0, 1).start()
    for copy in others[:3]:
        copy.start()
    local[0].wait()
    y_copy(0, 0).start()
    others[3].start()

    for label in range(REACH):
        inverse[label] = n
        inverse[n + REACH + label] = n

    def slot_at(at):
        row = lax.rem(z + depth - at // 4, depth)
        column = lax.rem(y + lax.rem(at // 2, 2), 2)
        return (row * 2 + column) * 2 + lax.rem(core + lax.rem(at, 2), 2)

    def invert(label, carry):
        found = lax.fori_loop(
            0, n, lambda slot, seen: jnp.maximum(seen, jnp.where(slots[slot_at(slot)] == label, slot, 0)), jnp.int32(0)
        )
        inverse[label + REACH] = found
        return carry

    lax.fori_loop(0, n, invert, 0)

    def clear(term, carry):
        half[n, term] = jnp.zeros((size, size), half.dtype)
        return carry

    lax.fori_loop(0, 2 * terms, clear, 0)

    row_of = lax.broadcasted_iota(jnp.int32, (size, size), 0)
    col_of = lax.broadcasted_iota(jnp.int32, (size, size), 1)

    def live(slot):
        label = slots[slot]
        return (row_of < rows[label]) & (col_of < cols[label])

    def weight(term, slot):
        moved = slots[slot]
        if term < terms:
            return coef[term, jnp.clip(moved + shift[term], 0, n - 1)]
        return coef_b[term - terms, jnp.clip(moved + shift_b[term - terms], 0, n - 1)]

    def first_product(step, column):
        at = [place(step, column, which) for which in range(2)]
        slot = [slot_from(step, column, which) for which in range(2)]
        pair = jnp.concatenate(
            [
                jnp.where(live(slot[which]), states[at[which]].astype(jnp.float32), 0.0).astype(states.dtype)
                for which in range(2)
            ],
            axis=1,
        )
        for term in range(2 * terms):
            product = jnp.dot(lefts[term], pair, preferred_element_type=jnp.float32)
            for which in range(2):
                half[at[which], term] = (
                    product[:, which * size:(which + 1) * size] * weight(term, slot[which])
                ).astype(half.dtype)

    z_copy(0, 1).wait_recv()
    y_copy(0, 1).start()
    local[1].wait()
    for copy in others[:3]:
        copy.wait_recv()
    landed = [
        pltpu.make_async_copy(shift_in, shift_b, local_sem.at[3]),
        pltpu.make_async_copy(coef_in, coef_b, local_sem.at[4]),
    ]
    for copy in landed:
        copy.start()
    for copy in landed:
        copy.wait()
    first_product(0, 0)

    def gather(step, carry):
        for which in range(2):
            z_copy(step, which).wait_recv()
            y_copy(step, which).start()
        first_product(step, 0)
        for which in range(2):
            y_copy(step - 1, which).wait_recv()
        first_product(step - 1, 1)
        return carry

    repeat(1, depth, gather, 0)
    for which in range(2):
        y_copy(depth - 1, which).wait_recv()
    first_product(depth - 1, 1)
    local[2].wait()
    others[3].wait_recv()

    group = 4

    def second_product(row, column):
        labels = [slots[slot_of(row, column, which)] for which in range(2)]
        total = None
        for begin in range(0, 2 * terms, group):
            picked = []
            for which in range(2):
                tiles = []
                for term in range(begin, begin + group):
                    moved = shift[term] if term < terms else shift_b[term - terms]
                    tiles.append(half[inverse[labels[which] - moved + REACH], term])
                picked.append(jnp.concatenate(tiles, axis=1))
            product = jnp.dot(
                jnp.concatenate(picked, axis=0),
                rights[begin:begin + group].reshape(group * size, size),
                preferred_element_type=jnp.float32,
            )
            total = product if total is None else total + product
        return total[:size], total[size:]

    def part_copy(step, which):
        at = step * 2 + which
        return remote(part_out.at[at], part_in.at[at], part_send.at[at], part_recv.at[at], neighbour)

    def sum_copy(step, which):
        at = step * 2 + which
        return remote(
            sum_out.at[at], sum_in.at[at], sum_send.at[at], sum_recv.at[at], device(row_to(step), 0, which)
        )

    def scatter_y(step, carry):
        for which, part in enumerate(second_product(row_to(step), 1)):
            part_out[step * 2 + which] = part.astype(part_out.dtype)
            part_copy(step, which).start()
        return carry

    repeat(1, depth, scatter_y, 0)
    scatter_y(0, 0)

    def column_sum(step, which, part):
        part_copy(step, which).wait_recv()
        return part + part_in[step * 2 + which].astype(jnp.float32)

    def scatter_z(step, carry):
        for which, part in enumerate(second_product(row_to(step), 0)):
            sum_out[step * 2 + which] = column_sum(step, which, part).astype(sum_out.dtype)
            sum_copy(step, which).start()
        return carry

    repeat(1, depth, scatter_z, 0)
    parts = second_product(z, 0)
    sum_out[1] = column_sum(0, 1, parts[1]).astype(sum_out.dtype)
    sum_copy(0, 1).start()
    own = column_sum(0, 0, parts[0])

    def add_rows(which):
        def add(step, total):
            sum_copy(step, which).wait_recv()
            return total + sum_in[step * 2 + which].astype(jnp.float32)

        return add

    mine = live(me)
    out[0, core] = jnp.where(mine, repeat(1, depth, add_rows(0), own), 0.0).astype(out.dtype)
    sum_copy(0, 1).wait_recv()
    total = repeat(1, depth, add_rows(1), sum_in[1].astype(jnp.float32))
    out[0, 1 - core] = jnp.where(mine, total, 0.0).astype(out.dtype)

    for copy in others:
        copy.wait_send()
    z_copy(0, 1).wait_send()
    sum_copy(0, 1).wait_send()
    for which in range(2):
        y_copy(0, which).wait_send()
        part_copy(0, which).wait_send()

    def drain(step, carry):
        for which in range(2):
            z_copy(step, which).wait_send()
            y_copy(step, which).wait_send()
            part_copy(step, which).wait_send()
            sum_copy(step, which).wait_send()
        return carry

    repeat(1, depth, drain, 0)


def shards(n, wave, slots, rows, cols, left, right, coef, shift):
    terms, size = left.shape[0], left.shape[1]
    kept = wave.dtype
    smem = pl.BlockSpec(memory_space=pltpu.SMEM)
    anywhere = pl.BlockSpec(memory_space=pl.ANY)
    dma = pltpu.SemaphoreType.DMA
    return pl.pallas_call(
        functools.partial(sigma_kernel, n),
        out_shape=jax.ShapeDtypeStruct(wave.shape, kept),
        in_specs=[anywhere, smem, smem, smem, anywhere, anywhere, smem, smem, anywhere, anywhere],
        out_specs=pl.BlockSpec(memory_space=pltpu.VMEM),
        scratch_shapes=[
            pltpu.VMEM((2 * terms, size, size), kept),
            pltpu.VMEM((2 * terms, size, size), kept),
            pltpu.SMEM(coef.shape, coef.dtype),
            pltpu.SMEM(shift.shape, shift.dtype),
            pltpu.VMEM(coef.shape, coef.dtype),
            pltpu.VMEM(shift.shape, shift.dtype),
            pltpu.VMEM((n, size, size), kept),
            pltpu.VMEM((n + 1, 2 * terms, size, size), kept),
            pltpu.SMEM((n + 2 * REACH,), jnp.int32),
            pltpu.VMEM((n // 2, size, size), kept),
            pltpu.VMEM((n // 2, size, size), kept),
            pltpu.VMEM((n // 2, size, size), kept),
            pltpu.VMEM((n // 2, size, size), kept),
            dma((5,)), dma((4,)), dma((4,)),
            dma((n // 2,)), dma((n // 2,)), dma((n // 2,)), dma((n // 2,)),
            dma((n // 2,)), dma((n // 2,)), dma((n // 2,)), dma((n // 2,)),
        ],
        compiler_params=pltpu.CompilerParams(
            collective_id=0, has_side_effects=True, vmem_limit_bytes=56 * 1024 * 1024
        ),
    )(wave, slots, rows, cols, left, right, coef, shift, coef, shift)


def solution(mesh):
    return jax.shard_map(
        functools.partial(shards, mesh.shape["sec"]),
        mesh=mesh,
        in_specs=(
            P(("parts", "sec"), None, None, None),
            P("parts"),
            P("parts"),
            P("parts"),
            P(("parts", "sec"), None, None),
            P(("parts", "sec"), None, None),
            P(("parts", "sec"), None),
            P(("parts", "sec")),
        ),
        out_specs=P(("parts", "sec"), None, None, None),
        check_vma=False,
    )
```

time: 207 us -> 32.8 us (0.16)
  waiting for transfers between devices: 98 us -> 0 us
  other arithmetic: 54 us -> 0 us
  Pallas kernels: 0 us -> 30.8 us
  local copies, waits for them, and re-layouts: 25.9 us -> 1.47 us
  between operations: 15.4 us -> 0.01 us
  matrix products: 11.8 us -> 0 us
    reduce_scatter x1 -> x0, waiting for transfers between devices: 60.9 us -> none  [shards(): lax.psum_scatter(partial_sum, 'sec', scatter_dimension=0, tiled=True)]
    all_gather x1 -> x0, waiting for transfers between devices: 37 us -> none  [shards(): source_piece = lax.all_gather(masked, 'sec', axis=0, tiled=True)]
    scatter-add x8 -> x0, other arithmetic: 36.4 us -> none  [add_term(): accumulator.at[clipped].add(weight[:, None, None, None] * product_term)]
    pallas_call x0 -> x1, Pallas kernels: none -> 30.8 us  [shards(): pl.pallas_call(functools.partial(sigma_kernel, n), out_shape=jax.ShapeDty...]
    select_n x19 -> x0, other arithmetic: 14.2 us -> none  [the longest x8 5.27 us: add_term(): weight = jnp.where(inside, coeff_row[clipped], 0.0)]
    gather x13 -> x0, local copies, waits for them, and re-layouts: 12.7 us -> none  [the longest x8 5.25 us: add_term(): weight = jnp.where(inside, coeff_row[clipped], 0.0)]
    dot_general x8 -> x0, matrix products: 11.8 us -> none  [add_term(): jnp.einsum('svac,cd->svad', halfway, right_op, preferred_element_type=jnp...]
    dynamic_slice x9 -> x0, local copies, waits for them, and re-layouts: 5.96 us -> none  [the longest x8 4.66 us: shards(): updated, unused = lax.scan(add_term, start_sum, term_packs)]
  transfers between devices with their start and end apart: 2 -> 0, of which waited for: 2 -> 0; matrix products, arithmetic and copies ran while one was open for 2% -> 0% of each run, Pallas kernels for 0% -> 0%
where the time goes in v1:
time: 32.8 us; the launch traced here: 32.3 us
  Pallas kernels  30.8 us (94%)
  local copies, waits for them, and re-layouts  1.47 us (4%)
    pallas_call x1, Pallas kernels, shards(): pl.pallas_call(functools.partial(sigma_kernel, n), out_shape=jax.ShapeDty...  30.8 us
    unnamed x1, local copies, waits for them, and re-layouts  1.47 us

profile of v1, /device:TPU:0, one launch (start us, length us, event | category | flops | bytes accessed | tf_op | source)
XLA Modules:
  0.0 32.3 jit_solution(248913973968654783)
XLA Ops:
  0.0 30.8 %shard_map.82 = bf16[1,2,128,128]{3,2,1,0:T(8,128)(2,1)} custom-call(bf16[1,2,128,128]{3,2,1,0:T(8,128)(2,1)} %wave.1, s32[16]{0:T(128)} %slots.1, s32[16]{0:T(128)} %rows.1, s32[16]{0:T(128)} %cols.1, bf16[8,128,128]{2,1,0:T(8,128)(2,1)} %left.1, bf16[8,128,128]{2,1,0:T(8,128)(2,1)} %right.1, f32[8,16]{1,0:T(8,128)} %coef_far.1, s32[8]{0:T(128)} %shift_far.1, ...), custom_call_target="tpu_custom_call" | custom-call | tf_op jit(solution)/shard_map/pallas_call | solution.py:297
  30.8 1.5 %copy.10 = bf16[1,2,128,128]{3,2,1,0:T(8,128)(2,1)} copy(bf16[1,2,128,128]{3,2,1,0:T(8,128)(2,1)} %shard_map.82) | data formatting | bytes 131072

commit v2 on v1

--- a/solution.py
+++ b/solution.py
@@ -123,14 +123,25 @@
         column = lax.rem(y + lax.rem(at // 2, 2), 2)
         return (row * 2 + column) * 2 + lax.rem(core + lax.rem(at, 2), 2)
 
-    def invert(label, carry):
-        found = lax.fori_loop(
-            0, n, lambda slot, seen: jnp.maximum(seen, jnp.where(slots[slot_at(slot)] == label, slot, 0)), jnp.int32(0)
-        )
-        inverse[label + REACH] = found
-        return carry
-
-    lax.fori_loop(0, n, invert, 0)
+    if n > 16:
+        def invert(label, carry):
+            found = lax.fori_loop(
+                0, n, lambda slot, seen: jnp.maximum(seen, jnp.where(slots[slot_at(slot)] == label, slot, 0)), jnp.int32(0)
+            )
+            inverse[label + REACH] = found
+            return carry
+
+        lax.fori_loop(0, n, invert, 0)
+    else:
+        names = []
+        for at in range(n):
+            step, rest = at // 4, at % 4
+            names.append(slots[slot_from(step, rest // 2, rest % 2)])
+        for label in range(n):
+            found = jnp.int32(0)
+            for at in range(1, n):
+                found = jnp.where(names[at] == label, at, found)
+            inverse[label + REACH] = found
 
     def clear(term, carry):
         half[n, term] = jnp.zeros((size, size), half.dtype)

time: 32.8 us -> 30.1 us (0.918)
  Pallas kernels: 30.8 us -> 28.4 us
    pallas_call x1, Pallas kernels: 30.8 us -> 28.4 us  [shards(): pl.pallas_call(functools.partial(sigma_kernel, n), out_shape=jax.ShapeDty...]
where the time goes in v2:
time: 30.1 us; the launch traced here: 29.9 us
  Pallas kernels  28.4 us (94%)
  local copies, waits for them, and re-layouts  1.47 us (5%)
    pallas_call x1, Pallas kernels, shards(): pl.pallas_call(functools.partial(sigma_kernel, n), out_shape=jax.ShapeDty...  28.4 us
    unnamed x1, local copies, waits for them, and re-layouts  1.47 us

profile of v2, /device:TPU:0, one launch (start us, length us, event | category | flops | bytes accessed | tf_op | source)
XLA Modules:
  0.0 29.9 jit_solution(5764011940652905030)
XLA Ops:
  0.0 28.4 %shard_map.82 = bf16[1,2,128,128]{3,2,1,0:T(8,128)(2,1)} custom-call(bf16[1,2,128,128]{3,2,1,0:T(8,128)(2,1)} %wave.1, s32[16]{0:T(128)} %slots.1, s32[16]{0:T(128)} %rows.1, s32[16]{0:T(128)} %cols.1, bf16[8,128,128]{2,1,0:T(8,128)(2,1)} %left.1, bf16[8,128,128]{2,1,0:T(8,128)(2,1)} %right.1, f32[8,16]{1,0:T(8,128)} %coef_far.1, s32[8]{0:T(128)} %shift_far.1, ...), custom_call_target="tpu_custom_call" | custom-call | tf_op jit(solution)/shard_map/pallas_call | solution.py:308
  28.4 1.5 %copy.10 = bf16[1,2,128,128]{3,2,1,0:T(8,128)(2,1)} copy(bf16[1,2,128,128]{3,2,1,0:T(8,128)(2,1)} %shard_map.82) | data formatting | bytes 131072
